TPU v7x, 128 devices: a whole 4x4x4 slice. The times are simulated.
128 devices in a mesh: loader: 4 (over z_hi, core), centers: 32 (over y, z_lo, x).
Axes of the slice: x: 4, y: 4, z: 4 (z_hi: 2, z_lo: 2; z = z_hi * 2 + z_lo), core: 2. Of those that a mesh axis runs over, the one named last changes fastest.
Arguments:
- pool: bfloat16 [32768, 256], P('loader'), may hold values from -6 to 6
- batch_index: int32 [2048], replicated, may hold values from 0 to 32767
- targets: float32 [16, 2048], replicated, may hold values from -6 to 6
- centers: bfloat16 [1048576, 256], P(('loader', 'centers')), may hold values from -6 to 6
- weights: float32 [16, 1048576], P(None, ('loader', 'centers')), may hold values from -1.8 to 1.8
- nys_index: int32 [8192], P(('loader', 'centers')), may hold values from 0 to 8191, as said below
- eigvecs: float32 [8192, 128], P(('loader', 'centers')), may hold values from -0.0625 to 0.0625
- damping: float32 [128], replicated, may hold values from 1 to 30
Outputs:
- new_weights: float32 [16, 1048576], P(None, ('loader', 'centers'))
- predictions: float32 [16, 2048], replicated
Inputs may be any that keep to these rules, and one draw needn't show every extreme that they name: `nys_index`: each device's block of 64 entries names distinct local rows of that device's own 8192 centers; entry k lies in [k * 128, (k + 1) * 128); the first is 0 and the last 8191.
All inputs are finite; a program needn't handle non-finite values.
Results may differ from a plain program's by a relative error of at most 0.0049.
Values may be sent and summed in bfloat16 or wider, within the bound.
No kernel may reach another device: no remote copies, remote signals or barrier semaphores. Data moves between devices by JAX's collectives and lax.ppermute only.
A program may use at most 256 MiB of HBM per device.

v0:
```python
import math
import jax
import jax.numpy as jnp
from jax import lax
from jax.sharding import PartitionSpec as P

D = 256


def pick_rows(pool, wanted):
    held = pool.shape[0]
    local = wanted - lax.axis_index("loader") * held
    owned = (local >= 0) & (local < held)
    rows = pool[jnp.clip(local, 0, held - 1)]
    return jnp.where(owned[:, None], rows, jnp.zeros_like(rows))


def body(pool, batch_index, targets, centers, weights, nys_index, eigvecs, damping):
    total_rows = batch_index.shape[0]
    share = total_rows // lax.axis_size("centers")
    mine = lax.dynamic_slice_in_dim(batch_index, lax.axis_index("centers") * share, share)
    summed = lax.psum(pick_rows(pool, mine), "loader").astype(jnp.float32).astype(jnp.bfloat16)
    batch = lax.all_gather(summed, "centers", axis=0, tiled=True)
    cen_sq = jnp.sum(centers.astype(jnp.float32) * centers.astype(jnp.float32), axis=1)
    width = min(512, total_rows)

    def tile(rows):
        row_sq = jnp.sum(rows.astype(jnp.float32) * rows.astype(jnp.float32), axis=1)
        cross = jnp.dot(rows, centers.T, preferred_element_type=jnp.float32)
        dist_sq = row_sq[:, None] + cen_sq[None, :] - 2.0 * cross
        return jnp.exp(-4.0 * jnp.sqrt(dist_sq) / math.sqrt(D)).astype(jnp.bfloat16)

    kern = lax.map(tile, batch.reshape(total_rows // width, width, batch.shape[1]))
    kern = kern.reshape(total_rows, centers.shape[0])
    w_half = weights.astype(jnp.bfloat16)
    partial_value = lax.dot_general(
        w_half, kern, (((1,), (1,)), ((), ())), preferred_element_type=jnp.float32
    )
    predictions = lax.psum(partial_value, ("loader", "centers"))
    resid = (predictions - targets).astype(jnp.bfloat16)
    grad = jnp.dot(resid, kern, preferred_element_type=jnp.float32)
    grad_nys = grad[:, nys_index]
    local_coeff = jnp.dot(
        grad_nys, eigvecs, precision=lax.Precision.HIGHEST, preferred_element_type=jnp.float32
    )
    coeff = lax.psum(local_coeff, ("loader", "centers"))
    delta = jnp.dot(
        coeff * damping[None, :],
        eigvecs.T,
        precision=lax.Precision.HIGHEST,
        preferred_element_type=jnp.float32,
    )
    fresh = weights - 2.0 * grad
    fresh = fresh.at[:, nys_index].add(2.0 * delta)
    return (fresh, predictions)


def solution(mesh):
    return jax.shard_map(
        body,
        mesh=mesh,
        in_specs=(
            P("loader", None),
            P(),
            P(),
            P(("loader", "centers"), None),
            P(None, ("loader", "centers")),
            P(("loader", "centers")),
            P(("loader", "centers"), None),
            P(),
        ),
        out_specs=(P(None, ("loader", "centers")), P()),
        check_vma=False,
    )
```

profile of v0, /device:TPU:1, one launch (start us, length us, event | category | flops | bytes accessed | tf_op | source)
XLA Modules:
  0.0 498.1 jit_solution(4399989665971109694)
XLA Ops:
  7.2 0.0 copy-start
  7.2 0.0 all-gather.2.cloned.1.call-start
  7.2 0.8 compare_select_fusion.1
  8.0 0.8 compare_and_fusion
  8.8 3.4 gather_fusion
  12.2 0.1 broadcast_select_fusion
  12.2 15.6 %psum.21 = bf16[64,256]{1,0:T(8,128)(2,1)} all-reduce(bf16[64,256]{1,0:T(8,128)(2,1)S(1)} %broadcast_select_fusion), channel_id=1, replica_groups=mesh['loader'=4,'centers'=32] {'loader'}, use_global_device_ids=true, to_apply=%region_0.1 | all-reduce | flops 16384 | bytes 65536 | tf_op jit(solution)/shard_map/psum | solution.py:22
  27.9 0.0 all-gather.2.cloned.1.call-update
  27.9 0.0 all-reduce.2.cloned.1.call-start
  28.0 0.7 compare_select_fusion
  28.6 3.3 multiply_reduce_fusion.1
  32.0 127.5 %all-gather.2.cloned.1.call-done = bf16[2048,256]{1,0:T(8,128)(2,1)} async-done(((bf16[64,256]{1,0:T(8,128)(2,1)}), bf16[2048,256]{1,0:T(8,128)(2,1)}) %all-gather.2.cloned.1.call-update) | async-done | bytes 1048592 | tf_op jit(solution)/shard_map/all_gather | solution.py:23
  159.5 0.0 copy-start.1
  159.5 58.4 %while.12 = (s32[]{:T(128)}, bf16[4,512,8192]{2,1,0:T(8,128)(2,1)}, bf16[4,512,256]{2,1,0:T(8,128)(2,1)}, f32[8192]{0:T(1024)S(1)}, bf16[8192,256]{1,0:T(8,128)(2,1)}, /*index=5*/s32[]{:T(128)}) while((s32[]{:T(128)}, bf16[4,512,8192]{2,1,0:T(8,128)(2,1)}, bf16[4,512,256]{2,1,0:T(8,128)(2,1)}, f32[8192]{0:T(1024)S(1)}, ...), condition=%wide.region_4.5_spmd, body=%wide.region_2.4_spmd.sunk | while | flops 2168847872 | bytes 13145161 | solution.py:33
  159.5 1.2 multiply_reduce_fusion.3
  160.6 13.5 %fusion.22 = bf16[4,512,8192]{2,1,0:T(8,128)(2,1)} fusion(bf16[4,512,8192]{2,1,0:T(8,128)(2,1)} %get-tuple-element.120, s32[]{:T(128)} %get-tuple-element.119, bf16[8192,256]{1,0:T(8,128)(2,1)} %get-tuple-element.129, f32[8192]{0:T(1024)S(1)} %get-tuple-element.128, f32[512]{0:T(512)S(1)} %multiply_reduce_fusion.3, ...), kind=kOutput, calls=%fused_computation.5.clone.1 | convolution fusion | flops 2168455168 | bytes 12880896 | tf_op jit(solution)/shard_map/while/body/eval_jaxpr/dot_general | solution.py:29
  174.1 1.1 multiply_reduce_fusion.3
  175.2 13.5 %fusion.22 = bf16[4,512,8192]{2,1,0:T(8,128)(2,1)} fusion(bf16[4,512,8192]{2,1,0:T(8,128)(2,1)} %get-tuple-element.120, s32[]{:T(128)} %get-tuple-element.119, bf16[8192,256]{1,0:T(8,128)(2,1)} %get-tuple-element.129, f32[8192]{0:T(1024)S(1)} %get-tuple-element.128, f32[512]{0:T(512)S(1)} %multiply_reduce_fusion.3, ...), kind=kOutput, calls=%fused_computation.5.clone.1 | convolution fusion | flops 2168455168 | bytes 12880896 | tf_op jit(solution)/shard_map/while/body/eval_jaxpr/dot_general | solution.py:29
  188.7 1.1 multiply_reduce_fusion.3
  189.8 13.5 %fusion.22 = bf16[4,512,8192]{2,1,0:T(8,128)(2,1)} fusion(bf16[4,512,8192]{2,1,0:T(8,128)(2,1)} %get-tuple-element.120, s32[]{:T(128)} %get-tuple-element.119, bf16[8192,256]{1,0:T(8,128)(2,1)} %get-tuple-element.129, f32[8192]{0:T(1024)S(1)} %get-tuple-element.128, f32[512]{0:T(512)S(1)} %multiply_reduce_fusion.3, ...), kind=kOutput, calls=%fused_computation.5.clone.1 | convolution fusion | flops 2168455168 | bytes 12880896 | tf_op jit(solution)/shard_map/while/body/eval_jaxpr/dot_general | solution.py:29
  203.3 1.1 multiply_reduce_fusion.3
  204.4 13.5 %fusion.22 = bf16[4,512,8192]{2,1,0:T(8,128)(2,1)} fusion(bf16[4,512,8192]{2,1,0:T(8,128)(2,1)} %get-tuple-element.120, s32[]{:T(128)} %get-tuple-element.119, bf16[8192,256]{1,0:T(8,128)(2,1)} %get-tuple-element.129, f32[8192]{0:T(1024)S(1)} %get-tuple-element.128, f32[512]{0:T(512)S(1)} %multiply_reduce_fusion.3, ...), kind=kOutput, calls=%fused_computation.5.clone.1 | convolution fusion | flops 2168455168 | bytes 12880896 | tf_op jit(solution)/shard_map/while/body/eval_jaxpr/dot_general | solution.py:29
  217.9 0.0 copy-done.1
  217.9 0.0 copy-start.3
  217.9 15.7 %convolution_bitcast_fusion = f32[16,2048]{1,0:T(8,128)} fusion(bf16[2048,8192]{1,0:T(8,128)(2,1)} %bitcast.28, f32[16,8192]{1,0:T(8,128)S(1)} %copy-done.1), kind=kOutput, calls=%fused_computation.11 | convolution fusion | flops 537001984 | bytes 34209792 | tf_op jit(solution)/shard_map/dot_general | solution.py:36
  233.6 0.0 all-reduce.2.cloned.1.call-update
  233.6 0.0 copy-start.4
  233.6 161.8 %all-reduce.2.cloned.1.call-done = f32[16,2048]{1,0:T(8,128)} async-done(((f32[16,2048]{1,0:T(8,128)}), f32[16,2048]{1,0:T(8,128)}) %all-reduce.2.cloned.1.call-update) | async-done | bytes 131088 | tf_op jit(solution)/shard_map/psum | solution.py:39
  395.4 0.0 copy-done.3
  395.4 0.0 copy-start.2
  395.4 14.8 %multiply_subtract_fusion = (f32[16,8192]{1,0:T(8,128)S(1)}, f32[16,8192]{1,0:T(8,128)S(1)}) fusion(f32[16,8192]{1,0:T(8,128)S(1)} %copy-done.1, bf16[2048,8192]{1,0:T(8,128)(2,1)} %bitcast.29, f32[16,2048]{1,0:T(8,128)} %all-reduce.2.cloned.1.call-done, f32[16,2048]{1,0:T(8,128)S(1)} %copy-done.3), kind=kOutput, calls=%fused_computation.14 | convolution fusion | flops 537198592 | bytes 35389440 | tf_op jit(solution)/shard_map/dot_general | solution.py:41
  410.3 2.6 copy.10
  412.9 2.8 gather_fusion.1
  415.7 0.0 copy-done
  415.7 0.2 fusion.10
  415.9 63.4 %psum.23 = f32[16,128]{1,0:T(8,128)S(1)} all-reduce(f32[16,128]{1,0:T(8,128)S(1)} %fusion.10), channel_id=1, replica_groups=mesh['loader'=4,'centers'=32] {'loader','centers'}, use_global_device_ids=true, to_apply=%region_6.7 | all-reduce | flops 2048 | bytes 16384 | tf_op jit(solution)/shard_map/psum | solution.py:46
  479.3 0.0 copy-done.4
  479.3 0.1 fusion.5
  479.4 0.1 copy.12
  479.5 2.6 copy.11
  482.1 4.9 scatter_fusion
  487.1 3.5 copy.13
  490.6 0.0 copy-done.2
  490.6 0.7 copy.25
  (3 shorter events, 0.0 us)
Async XLA Ops:
  7.2 408.5 %copy-start = (f32[64,128]{1,0:T(8,128)S(1)}, f32[64,128]{1,0:T(8,128)}, u32[]{:S(2)}) copy-start(f32[64,128]{1,0:T(8,128)} %param.16) | copy-start | bytes 98308
  7.2 152.3 %all-gather.2.cloned.1.call-start = ((), (), s32[]{:S(2)}) async-start(), calls=%async_computation | async-start | bytes 1081344 | tf_op jit(solution)/shard_map/all_gather | solution.py:23
  27.9 367.5 %all-reduce.2.cloned.1.call-start = ((), (), s32[]{:S(2)}) async-start(), calls=%async_computation.1 | async-start | bytes 262144 | tf_op jit(solution)/shard_map/psum | solution.py:39
  159.5 58.4 %copy-start.1 = (f32[16,8192]{1,0:T(8,128)S(1)}, f32[16,8192]{1,0:T(8,128)}, u32[]{:S(2)}) copy-start(f32[16,8192]{1,0:T(8,128)} %param.14) | copy-start | bytes 1572868
  217.9 177.5 %copy-start.3 = (f32[16,2048]{1,0:T(8,128)S(1)}, f32[16,2048]{1,0:T(8,128)}, u32[]{:S(2)}) copy-start(f32[16,2048]{1,0:T(8,128)} %param.12) | copy-start | bytes 393220
  233.6 245.7 %copy-start.4 = (f32[128]{0:T(128)S(1)}, f32[128]{0:T(128)}, u32[]{:S(2)}) copy-start(f32[128]{0:T(128)} %param.17) | copy-start | bytes 1540
  395.4 95.2 %copy-start.2 = (f32[16,2048]{1,0:T(8,128)S(1)}, f32[16,2048]{1,0:T(8,128)}, u32[]{:S(2)}) copy-start(f32[16,2048]{1,0:T(8,128)} %all-reduce.2.cloned.1.call-done) | copy-start | bytes 393220
Sparse Core Ops, SparseCore 0:
  28.0 131.4 all-gather.1
  233.7 161.6 all-reduce.1
where the time goes:
time: 499 us; the launch traced here: 498 us
  waiting for transfers between devices  289 us (58%)
  matrix products  84.8 us (17%)
  blocking collectives  79.1 us (16%)
  local copies, waits for them, and re-layouts  15.7 us (3%)
  other arithmetic  15 us (3%)
  between operations  14.1 us (3%)
    psum x1, waiting for transfers between devices, body(): predictions = lax.psum(partial_value, ('loader', 'centers'))  162 us
    all_gather x1, waiting for transfers between devices, body(): batch = lax.all_gather(summed, 'centers', axis=0, tiled=True)  128 us
    psum x1, blocking collectives, body(): coeff = lax.psum(local_coeff, ('loader', 'centers'))  63.4 us
    dot_general x4, matrix products, tile(): cross = jnp.dot(rows, centers.T, preferred_element_type=jnp.float32)  54 us
    dot_general x1, matrix products, body(): lax.dot_general(w_half, kern, (((1,), (1,)), ((), ())), preferred_element...  15.7 us
    psum x1, blocking collectives, body(): lax.psum(pick_rows(pool, mine), 'loader').astype(jnp.float32)  15.6 us
    dot_general x1, matrix products, body(): grad = jnp.dot(resid, kern, preferred_element_type=jnp.float32)  14.8 us
  transfers between devices with their start and end apart: 2, of which 2 were waited for; matrix products, arithmetic and copies ran while one was open for 1% of the time, Pallas kernels for 0%

commit v1 on v0

--- a/solution.py
+++ b/solution.py
@@ -43,7 +43,7 @@
     local_coeff = jnp.dot(
         grad_nys, eigvecs, precision=lax.Precision.HIGHEST, preferred_element_type=jnp.float32
     )
-    coeff = lax.psum(local_coeff, ("loader", "centers"))
+    coeff = lax.psum(lax.psum(local_coeff, axis_name="centers"), axis_name="loader")
     delta = jnp.dot(
         coeff * damping[None, :],
         eigvecs.T,

time: 499 us -> 523 us (1.048)
  blocking collectives: 79.1 us -> 103 us
    psum x1 -> x2, blocking collectives: 63.4 us -> 87.6 us  [the longest x1 66.8 us: body(): lax.psum(local_coeff, axis_name='centers')]
where the time goes in v1:
time: 523 us; the launch traced here: 522 us
  waiting for transfers between devices  289 us (55%)
  blocking collectives  103 us (20%)
  matrix products  84.8 us (16%)
  local copies, waits for them, and re-layouts  15.7 us (3%)
  other arithmetic  15 us (3%)
  between operations  14.1 us (3%)
    psum x1, waiting for transfers between devices, body(): predictions = lax.psum(partial_value, ('loader', 'centers'))  162 us
    all_gather x1, waiting for transfers between devices, body(): batch = lax.all_gather(summed, 'centers', axis=0, tiled=True)  128 us
    psum x1, blocking collectives, body(): lax.psum(local_coeff, axis_name='centers')  66.8 us
    dot_general x4, matrix products, tile(): cross = jnp.dot(rows, centers.T, preferred_element_type=jnp.float32)  54 us
    psum x1, blocking collectives, body(): lax.psum(lax.psum(local_coeff, axis_name='centers'), axis_name='loader')  20.8 us
    dot_general x1, matrix products, body(): lax.dot_general(w_half, kern, (((1,), (1,)), ((), ())), preferred_element...  15.7 us
    psum x1, blocking collectives, body(): lax.psum(pick_rows(pool, mine), 'loader').astype(jnp.float32)  15.6 us
    dot_general x1, matrix products, body(): grad = jnp.dot(resid, kern, preferred_element_type=jnp.float32)  14.8 us
  transfers between devices with their start and end apart: 2, of which 2 were waited for; matrix products, arithmetic and copies ran while one was open for 1% of the time, Pallas kernels for 0%

profile of v1, /device:TPU:1, one launch (start us, length us, event | category | flops | bytes accessed | tf_op | source)
XLA Modules:
  0.0 522.3 jit_solution(1734618508663912807)
XLA Ops:
  7.2 0.0 copy-start
  7.2 0.0 all-gather.2.cloned.1.call-start
  7.2 0.8 compare_select_fusion.1
  8.0 0.8 compare_and_fusion
  8.8 3.4 gather_fusion
  12.2 0.1 broadcast_select_fusion
  12.2 15.6 %psum.28 = bf16[64,256]{1,0:T(8,128)(2,1)} all-reduce(bf16[64,256]{1,0:T(8,128)(2,1)S(1)} %broadcast_select_fusion), channel_id=1, replica_groups=mesh['loader'=4,'centers'=32] {'loader'}, use_global_device_ids=true, to_apply=%region_0.1 | all-reduce | flops 16384 | bytes 65536 | tf_op jit(solution)/shard_map/psum | solution.py:22
  27.9 0.0 all-gather.2.cloned.1.call-update
  27.9 0.0 all-reduce.2.cloned.1.call-start
  28.0 0.7 compare_select_fusion
  28.6 3.3 multiply_reduce_fusion.1
  32.0 127.5 %all-gather.2.cloned.1.call-done = bf16[2048,256]{1,0:T(8,128)(2,1)} async-done(((bf16[64,256]{1,0:T(8,128)(2,1)}), bf16[2048,256]{1,0:T(8,128)(2,1)}) %all-gather.2.cloned.1.call-update) | async-done | bytes 1048592 | tf_op jit(solution)/shard_map/all_gather | solution.py:23
  159.5 0.0 copy-start.1
  159.5 58.4 %while.12 = (s32[]{:T(128)}, bf16[4,512,8192]{2,1,0:T(8,128)(2,1)}, bf16[4,512,256]{2,1,0:T(8,128)(2,1)}, f32[8192]{0:T(1024)S(1)}, bf16[8192,256]{1,0:T(8,128)(2,1)}, /*index=5*/s32[]{:T(128)}) while((s32[]{:T(128)}, bf16[4,512,8192]{2,1,0:T(8,128)(2,1)}, bf16[4,512,256]{2,1,0:T(8,128)(2,1)}, f32[8192]{0:T(1024)S(1)}, ...), condition=%wide.region_4.5_spmd, body=%wide.region_2.4_spmd.sunk | while | flops 2168847872 | bytes 13145161 | solution.py:33
  159.5 1.2 multiply_reduce_fusion.3
  160.6 13.5 %fusion.22 = bf16[4,512,8192]{2,1,0:T(8,128)(2,1)} fusion(bf16[4,512,8192]{2,1,0:T(8,128)(2,1)} %get-tuple-element.120, s32[]{:T(128)} %get-tuple-element.119, bf16[8192,256]{1,0:T(8,128)(2,1)} %get-tuple-element.129, f32[8192]{0:T(1024)S(1)} %get-tuple-element.128, f32[512]{0:T(512)S(1)} %multiply_reduce_fusion.3, ...), kind=kOutput, calls=%fused_computation.5.clone.1 | convolution fusion | flops 2168455168 | bytes 12880896 | tf_op jit(solution)/shard_map/while/body/eval_jaxpr/dot_general | solution.py:29
  174.1 1.1 multiply_reduce_fusion.3
  175.2 13.5 %fusion.22 = bf16[4,512,8192]{2,1,0:T(8,128)(2,1)} fusion(bf16[4,512,8192]{2,1,0:T(8,128)(2,1)} %get-tuple-element.120, s32[]{:T(128)} %get-tuple-element.119, bf16[8192,256]{1,0:T(8,128)(2,1)} %get-tuple-element.129, f32[8192]{0:T(1024)S(1)} %get-tuple-element.128, f32[512]{0:T(512)S(1)} %multiply_reduce_fusion.3, ...), kind=kOutput, calls=%fused_computation.5.clone.1 | convolution fusion | flops 2168455168 | bytes 12880896 | tf_op jit(solution)/shard_map/while/body/eval_jaxpr/dot_general | solution.py:29
  188.7 1.1 multiply_reduce_fusion.3
  189.8 13.5 %fusion.22 = bf16[4,512,8192]{2,1,0:T(8,128)(2,1)} fusion(bf16[4,512,8192]{2,1,0:T(8,128)(2,1)} %get-tuple-element.120, s32[]{:T(128)} %get-tuple-element.119, bf16[8192,256]{1,0:T(8,128)(2,1)} %get-tuple-element.129, f32[8192]{0:T(1024)S(1)} %get-tuple-element.128, f32[512]{0:T(512)S(1)} %multiply_reduce_fusion.3, ...), kind=kOutput, calls=%fused_computation.5.clone.1 | convolution fusion | flops 2168455168 | bytes 12880896 | tf_op jit(solution)/shard_map/while/body/eval_jaxpr/dot_general | solution.py:29
  203.3 1.1 multiply_reduce_fusion.3
  204.4 13.5 %fusion.22 = bf16[4,512,8192]{2,1,0:T(8,128)(2,1)} fusion(bf16[4,512,8192]{2,1,0:T(8,128)(2,1)} %get-tuple-element.120, s32[]{:T(128)} %get-tuple-element.119, bf16[8192,256]{1,0:T(8,128)(2,1)} %get-tuple-element.129, f32[8192]{0:T(1024)S(1)} %get-tuple-element.128, f32[512]{0:T(512)S(1)} %multiply_reduce_fusion.3, ...), kind=kOutput, calls=%fused_computation.5.clone.1 | convolution fusion | flops 2168455168 | bytes 12880896 | tf_op jit(solution)/shard_map/while/body/eval_jaxpr/dot_general | solution.py:29
  217.9 0.0 copy-done.1
  217.9 0.0 copy-start.3
  217.9 15.7 %convolution_bitcast_fusion = f32[16,2048]{1,0:T(8,128)} fusion(bf16[2048,8192]{1,0:T(8,128)(2,1)} %bitcast.28, f32[16,8192]{1,0:T(8,128)S(1)} %copy-done.1), kind=kOutput, calls=%fused_computation.11 | convolution fusion | flops 537001984 | bytes 34209792 | tf_op jit(solution)/shard_map/dot_general | solution.py:36
  233.6 0.0 all-reduce.2.cloned.1.call-update
  233.6 0.0 copy-start.4
  233.6 161.8 %all-reduce.2.cloned.1.call-done = f32[16,2048]{1,0:T(8,128)} async-done(((f32[16,2048]{1,0:T(8,128)}), f32[16,2048]{1,0:T(8,128)}) %all-reduce.2.cloned.1.call-update) | async-done | bytes 131088 | tf_op jit(solution)/shard_map/psum | solution.py:39
  395.4 0.0 copy-done.3
  395.4 0.0 copy-start.2
  395.4 14.8 %multiply_subtract_fusion = (f32[16,8192]{1,0:T(8,128)S(1)}, f32[16,8192]{1,0:T(8,128)S(1)}) fusion(f32[16,8192]{1,0:T(8,128)S(1)} %copy-done.1, bf16[2048,8192]{1,0:T(8,128)(2,1)} %bitcast.29, f32[16,2048]{1,0:T(8,128)} %all-reduce.2.cloned.1.call-done, f32[16,2048]{1,0:T(8,128)S(1)} %copy-done.3), kind=kOutput, calls=%fused_computation.14 | convolution fusion | flops 537198592 | bytes 35389440 | tf_op jit(solution)/shard_map/dot_general | solution.py:41
  410.3 2.6 copy.10
  412.9 2.8 gather_fusion.1
  415.7 0.0 copy-done
  415.7 0.2 fusion.10
  415.9 66.8 %psum.30 = f32[16,128]{1,0:T(8,128)S(1)} all-reduce(f32[16,128]{1,0:T(8,128)S(1)} %fusion.10), channel_id=1, replica_groups=mesh['loader'=4,'centers'=32] {'centers'}, use_global_device_ids=true, to_apply=%region_6.7 | all-reduce | flops 2048 | bytes 16384 | tf_op jit(solution)/shard_map/psum | solution.py:46
  482.6 20.8 %psum.31 = f32[16,128]{1,0:T(8,128)S(1)} all-reduce(f32[16,128]{1,0:T(8,128)S(1)} %psum.30), channel_id=1, replica_groups=mesh['loader'=4,'centers'=32] {'loader'}, use_global_device_ids=true, to_apply=%region_7.8 | all-reduce | flops 2048 | bytes 16384 | tf_op jit(solution)/shard_map/psum | solution.py:46
  503.5 0.0 copy-done.4
  503.5 0.1 fusion.5
  503.6 0.1 copy.12
  503.7 2.6 copy.11
  506.3 4.9 scatter_fusion
  511.3 3.5 copy.13
  514.8 0.0 copy-done.2
  514.8 0.7 copy.25
  (3 shorter events, 0.0 us)
Async XLA Ops:
  7.2 408.5 %copy-start = (f32[64,128]{1,0:T(8,128)S(1)}, f32[64,128]{1,0:T(8,128)}, u32[]{:S(2)}) copy-start(f32[64,128]{1,0:T(8,128)} %param.16) | copy-start | bytes 98308
  7.2 152.3 %all-gather.2.cloned.1.call-start = ((), (), s32[]{:S(2)}) async-start(), calls=%async_computation | async-start | bytes 1081344 | tf_op jit(solution)/shard_map/all_gather | solution.py:23
  27.9 367.5 %all-reduce.2.cloned.1.call-start = ((), (), s32[]{:S(2)}) async-start(), calls=%async_computation.1 | async-start | bytes 262144 | tf_op jit(solution)/shard_map/psum | solution.py:39
  159.5 58.4 %copy-start.1 = (f32[16,8192]{1,0:T(8,128)S(1)}, f32[16,8192]{1,0:T(8,128)}, u32[]{:S(2)}) copy-start(f32[16,8192]{1,0:T(8,128)} %param.14) | copy-start | bytes 1572868
  217.9 177.5 %copy-start.3 = (f32[16,2048]{1,0:T(8,128)S(1)}, f32[16,2048]{1,0:T(8,128)}, u32[]{:S(2)}) copy-start(f32[16,2048]{1,0:T(8,128)} %param.12) | copy-start | bytes 393220
  233.6 269.9 %copy-start.4 = (f32[128]{0:T(128)S(1)}, f32[128]{0:T(128)}, u32[]{:S(2)}) copy-start(f32[128]{0:T(128)} %param.17) | copy-start | bytes 1540
  395.4 119.3 %copy-start.2 = (f32[16,2048]{1,0:T(8,128)S(1)}, f32[16,2048]{1,0:T(8,128)}, u32[]{:S(2)}) copy-start(f32[16,2048]{1,0:T(8,128)} %all-reduce.2.cloned.1.call-done) | copy-start | bytes 393220
Sparse Core Ops, SparseCore 0:
  28.0 131.4 all-gather.1
  233.7 161.6 all-reduce.1
